TPU v7x, 32 devices: a whole 2x2x4 slice. The times are simulated.
32 devices in a mesh: tm: 16 (over z, y, core), space: 2 (over x).
Axes of the slice: x: 2, y: 2, z: 4, core: 2. Of those that a mesh axis runs over, the one named last changes fastest.
Arguments:
- start_states: float32 [16, 64, 256], P('tm', 'space'), may hold values from -6 to 6
- region_map: int32 [64, 256], P('space'), may hold values from 0 to 3
- source: float32 [2, 64, 256], P(None, 'space'), may hold values from -6 to 6
- front: int32 [], replicated, may hold values from 9 to 15
Outputs:
- new_states: float32 [16, 64, 256], P('tm', 'space')
- jumps: float32 [16, 64, 256], P('tm', 'space')
All inputs are finite; a program needn't handle non-finite values.
Results may differ from a plain program's by a relative error of at most 0.000027.
Values sent between devices are 32-bit elements; how exact they have to be, the bound alone decides.
A program may use at most 64 MiB of HBM per device.

v0:
```python
import functools
import math

import jax
import jax.numpy as jnp
from jax import lax
from jax.experimental import pallas as pl
from jax.experimental.pallas import tpu as pltpu
from jax.sharding import PartitionSpec as P

FINE = 16
ITERS = 2
GROUP = 4
DECAY_AT = 5
PRODUCT_AT = 11
TILE = 8
LANES = 128

RELUCTIVITY = (1.0, 0.3, 1.0, 0.25)
SATURATION = (0.0, 2.0, 0.0, 1.5)
MOBILITY = (0.15, 0.02, 0.0004, 0.0008)

MESH = pl.DeviceIdType.MESH


def lookup(region, table):
    result = jnp.zeros(region.shape, jnp.float32)
    for code, entry in enumerate(table):
        result = jnp.where(region == code, jnp.float32(entry), result)
    return result


def inverse(x):
    return pl.reciprocal(x, approx=True)


def grid(slices):
    t = lax.axis_index("tm")
    return t, lax.axis_index("space"), t // GROUP, t % GROUP, slices // GROUP


def send_to(src, dst, send, recv, tm, space):
    return pltpu.make_async_remote_copy(
        src_ref=src, dst_ref=dst, send_sem=send, recv_sem=recv,
        device_id={"tm": tm, "space": space}, device_id_type=MESH,
    )


def edge_kernel(
    strips, rows, up_base,
    states_in, region_in, source_in,
    field_out, region_out, source_out,
    field, region, source, local_sem, edge_send, edge_recv,
):
    t, x = lax.axis_index("tm"), lax.axis_index("space")
    has_up = x > 0
    has_down = x < strips - 1
    halo = FINE
    barrier = pltpu.get_barrier_semaphore()

    def greet(space):
        pl.semaphore_signal(
            barrier, inc=1, device_id={"tm": t, "space": space}, device_id_type=MESH
        )

    @pl.when(has_up)
    def _():
        greet(x - 1)

    @pl.when(has_down)
    def _():
        greet(x + 1)

    own = pl.ds(0, rows)
    loads = [
        pltpu.make_async_copy(states_in.at[0], field.at[own], local_sem.at[0]),
        pltpu.make_async_copy(region_in, region.at[own], local_sem.at[1]),
        pltpu.make_async_copy(source_in, source.at[:, own], local_sem.at[2]),
    ]
    for copy in loads:
        copy.start()
    for copy in loads:
        copy.wait()
    pl.semaphore_wait(barrier, has_up.astype(jnp.int32) + has_down.astype(jnp.int32))

    def edge_copies(way):
        src = pl.ds(0, halo) if way == 0 else pl.ds(rows - halo, halo)
        dst = pl.ds(rows, halo) if way == 0 else pl.ds(up_base, halo)
        to = x - 1 if way == 0 else x + 1
        send, recv = edge_send.at[way], edge_recv.at[way]
        return [
            send_to(source.at[:, src], source.at[:, dst], send.at[2], recv.at[2], t, to),
            send_to(region.at[src], region.at[dst], send.at[0], recv.at[0], t, to),
            send_to(field.at[src], field.at[dst], send.at[1], recv.at[1], t, to),
        ]

    @pl.when(has_up)
    def _():
        for copy in edge_copies(0):
            copy.start()

    @pl.when(has_down)
    def _():
        for copy in edge_copies(1):
            copy.start()

    field_out[own] = field[own]
    region_out[own] = region[own]
    source_out[:, own] = source[:, own]

    @pl.when(has_down)
    def _():
        for copy in edge_copies(0):
            copy.wait_recv()
        at = pl.ds(rows, halo)
        field_out[at] = field[at]
        region_out[at] = region[at]
        source_out[:, at] = source[:, at]

    @pl.when(has_up)
    def _():
        for copy in edge_copies(1):
            copy.wait_recv()
        at = pl.ds(up_base, halo)
        field_out[at] = field[at]
        region_out[at] = region[at]
        source_out[:, at] = source[:, at]

    @pl.when(has_up)
    def _():
        for copy in edge_copies(0):
            copy.wait_send()

    @pl.when(has_down)
    def _():
        for copy in edge_copies(1):
            copy.wait_send()


def kernel(
    slices, strips, rows, cols, up_base, total_rows,
    begin, region, source, front_ref,
    ends_out,
    field, coef_a, coef_b, drive,
    decay_own, decay_all, offset_own, offset_all,
    prod_own, prod_all, shift_own, shift_all, solved, end_own, end_prev,
    group_send, group_recv, level_send, level_recv,
    back_send, back_recv, halo_send, halo_recv, end_send, end_recv,
):
    t, x, level, g, levels = grid(slices)
    slab = rows // GROUP
    has_up = x > 0
    has_down = x < strips - 1
    halo = FINE
    groups = total_rows // TILE
    halves = cols // LANES

    def peer(j):
        return level * GROUP + (g + j) % GROUP

    def far(i):
        return ((level + i) % levels) * GROUP + g

    def remote(src, dst, send, recv, tm, space=None):
        return send_to(src, dst, send, recv, tm, x if space is None else space)

    barrier = pltpu.get_barrier_semaphore()

    def greet(tm, space):
        pl.semaphore_signal(
            barrier, inc=1, device_id={"tm": tm, "space": space}, device_id_type=MESH
        )

    expected = (GROUP - 1) + (levels - 1) + 2

    @pl.when(has_up)
    def _():
        for j in range(GROUP):
            greet(peer(j), x - 1)

    @pl.when(has_down)
    def _():
        for j in range(GROUP):
            greet(peer(j), x + 1)

    for j in range(1, GROUP):
        greet(peer(j), x)
    for i in range(1, levels):
        greet(far(i), x)
    greet((t + 1) % slices, x)
    greet((t + slices - 1) % slices, x)

    own = pl.ds(0, rows)
    cos0, sin0 = jnp.float32(1.0), jnp.float32(0.0)
    for b in range(max(1, (slices - 1).bit_length())):
        on = (t // (1 << b)) % 2 == 1
        angle = 2.0 * math.pi * (1 << b) / slices
        cb = jnp.where(on, jnp.float32(math.cos(angle)), jnp.float32(1.0))
        sb = jnp.where(on, jnp.float32(math.sin(angle)), jnp.float32(0.0))
        cos0, sin0 = cos0 * cb - sin0 * sb, sin0 * cb + cos0 * sb
    cos_d = math.cos(2.0 * math.pi / (slices * FINE))
    sin_d = math.sin(2.0 * math.pi / (slices * FINE))
    cut = lax.rem(front_ref[0] + (slices - 1), slices)
    keep = jnp.where(t == cut, jnp.float32(0.0), jnp.float32(1.0))

    count = expected + GROUP * (has_up.astype(jnp.int32) + has_down.astype(jnp.int32))
    sub = lax.broadcasted_iota(jnp.int32, (TILE, LANES), 0)
    lane = lax.broadcasted_iota(jnp.int32, (TILE, LANES), 1)
    top, bottom = sub == 0, sub == TILE - 1
    left, right = lane == 0, lane == LANES - 1
    own_groups = rows // TILE

    def neighbours(v):
        down_roll = [[pltpu.roll(a, 1, 0) for a in line] for line in v]
        up_roll = [[pltpu.roll(a, TILE - 1, 0) for a in line] for line in v]
        right_roll = [[pltpu.roll(a, 1, 1) for a in line] for line in v]
        left_roll = [[pltpu.roll(a, LANES - 1, 1) for a in line] for line in v]
        out = []
        for r in range(groups):
            line = []
            for h in range(halves):
                above = down_roll[r - 1][h]
                if r == 0:
                    above = jnp.where(has_up, above, 0.0)
                below = up_roll[(r + 1) % groups][h]
                if r == own_groups - 1:
                    below = jnp.where(has_down, below, 0.0)
                before = right_roll[r][h - 1] if h > 0 else 0.0
                after = left_roll[r][h + 1] if h < halves - 1 else 0.0
                line.append((
                    jnp.where(top, above, down_roll[r][h]),
                    jnp.where(bottom, below, up_roll[r][h]),
                    jnp.where(left, before, right_roll[r][h]),
                    jnp.where(right, after, left_roll[r][h]),
                ))
            out.append(line)
        return out

    def place(r, h):
        return pl.ds(r * TILE, TILE), pl.ds(h * LANES, LANES)

    def tiles(ref, count):
        return [[ref[place(r, h)] for h in range(halves)] for r in range(count)]

    codes = tiles(region, groups)
    relu = [[lookup(c, RELUCTIVITY) for c in line] for line in codes]
    satu = [[lookup(c, SATURATION) for c in line] for line in codes]
    relu_near, satu_near = neighbours(relu), neighbours(satu)
    for r in range(groups):
        for h in range(halves):
            mobile = lookup(codes[r][h], MOBILITY)
            at = place(r, h)
            for f in range(4):
                face_rel = 0.5 * (relu[r][h] + relu_near[r][h][f])
                face_sat = 0.5 * (satu[r][h] + satu_near[r][h][f])
                base = mobile * face_rel
                coef_b[f, *at] = base * face_sat
                coef_a[f, *at] = base + base * face_sat
            drive[0, *at] = mobile * source[0, *at]
            drive[1, *at] = mobile * source[1, *at]

    def step(v, cos_k, sin_k):
        near = neighbours(v)
        out, diagonals = [], []
        for r in range(groups):
            line, diag_line = [], []
            for h in range(halves):
                at = place(r, h)
                c = v[r][h]
                gain = drive[0, *at] * cos_k + drive[1, *at] * sin_k
                diagonal = None
                for f in range(4):
                    d = near[r][h][f] - c
                    q = coef_a[f, *at] - coef_b[f, *at] * inverse(1.0 + d * d)
                    gain = gain + q * d
                    diagonal = q if diagonal is None else diagonal + q
                line.append(c + gain)
                diag_line.append(diagonal)
            out.append(line)
            diagonals.append(diag_line)
        return out, diagonals

    def flat(v):
        return tuple(a for line in v for a in line)

    def nest(v):
        return [list(v[r * halves:(r + 1) * halves]) for r in range(groups)]

    mine = pl.ds(pl.multiple_of(g * slab, slab), slab)

    def group_copies(it, kind, src, dst):
        out = []
        for j in (2, 3, 1):
            to = (g + j) % GROUP
            out.append(remote(
                src.at[it, pl.ds(pl.multiple_of(to * slab, slab), slab)], dst.at[it, g],
                group_send.at[it, kind], group_recv.at[it, kind], peer(j),
            ))
        return out

    def group_all(it, kind, dst):
        part = dst.at[it, pl.ds(0, GROUP - 1)]
        return remote(part, part, group_send.at[it, kind], group_recv.at[it, kind], peer(1))

    def level_copies(it, kind, src, dst):
        return [
            remote(
                src.at[it], dst.at[it, levels - i - 1],
                level_send.at[it, kind], level_recv.at[it, kind], far(i),
            )
            for i in range(levels - 1, 0, -1)
        ]

    def level_all(it, kind, dst):
        part = dst.at[it]
        return remote(part, part, level_send.at[it, kind], level_recv.at[it, kind], far(1))

    def back_copies(it):
        return [
            remote(
                solved.at[it, (g + j) % GROUP], field.at[it + 1, mine],
                back_send.at[it], back_recv.at[it], peer(j),
            )
            for j in (2, 3, 1)
        ]

    def back_all(it):
        part = solved.at[it, pl.ds(0, GROUP - 1)]
        return remote(part, part, back_send.at[it], back_recv.at[it], peer(1))

    per_halo = halo // slab
    low = g < per_halo
    high = g >= GROUP - per_halo

    def halo_copies(it, way):
        if way == 0:
            start, to = rows + g * slab, x - 1
        else:
            start, to = up_base + (g - (GROUP - per_halo)) * slab, x + 1
        dst = pl.ds(pl.multiple_of(start, slab), slab)
        return [
            remote(
                solved.at[it, (g + j) % GROUP], field.at[it + 1, dst],
                halo_send.at[it, way], halo_recv.at[it, way], peer(j), to,
            )
            for j in (2, 3, 1, 0)
        ]

    def halo_sent(it, way):
        part = solved.at[it]
        return remote(part, part, halo_send.at[it, way], halo_recv.at[it, way], peer(1))

    def halo_here(it, way):
        part = field.at[it + 1, pl.ds(rows if way == 0 else up_base, halo)]
        return remote(part, part, halo_send.at[it, way], halo_recv.at[it, way], peer(1))

    def start_all(copies):
        for copy in copies:
            copy.start()

    def end_copy():
        return remote(end_own, end_prev, end_send, end_recv, (t + 1) % slices)

    for r in range(groups):
        for h in range(halves):
            field[0, *place(r, h)] = begin[place(r, h)]

    def sweep(it, _):
        more = it < ITERS - 1

        def turn(k, carry):
            v, cos_k, sin_k = carry
            v, diagonals = step(nest(v), cos_k, sin_k)

            @pl.when(k == 0)
            def _():
                for r in range(own_groups):
                    for h in range(halves):
                        decay_own[it, *place(r, h)] = keep / (1.0 + FINE * diagonals[r][h])

            @pl.when((it == 0) & (k == DECAY_AT))
            def _():
                pl.semaphore_wait(barrier, count)

            @pl.when(k == DECAY_AT)
            def _():
                start_all(group_copies(it, 0, decay_own, decay_all))
                decay_all[it, g] = decay_own[it, mine]

            @pl.when(k == PRODUCT_AT)
            def _():
                group_all(it, 0, decay_all).wait_recv()
                product = decay_all[it, 0]
                for j in range(1, GROUP):
                    product = product * decay_all[it, j]
                prod_own[it] = product
                start_all(level_copies(it, 0, prod_own, prod_all))

            return flat(v), cos_k * cos_d - sin_k * sin_d, sin_k * cos_d + cos_k * sin_d

        v, _, _ = lax.fori_loop(0, FINE, turn, (flat(tiles(field.at[it], groups)), cos0, sin0))
        v = nest(v)
        for r in range(own_groups):
            for h in range(halves):
                at = place(r, h)
                offset_own[it, *at] = v[r][h] - decay_own[it, *at] * field[it, *at]
                end_own[at] = v[r][h]
        start_all(group_copies(it, 1, offset_own, offset_all))
        offset_all[it, g] = offset_own[it, mine]

        @pl.when(jnp.logical_not(more))
        def _():
            end_copy().start()

        group_all(it, 1, offset_all).wait_recv()
        shift = offset_all[it, 0]
        for k in range(1, GROUP):
            shift = decay_all[it, k] * shift + offset_all[it, k]
        shift_own[it] = shift
        start_all(level_copies(it, 1, shift_own, shift_all))
        level_all(it, 0, prod_all).wait_recv()
        level_all(it, 1, shift_all).wait_recv()
        value = shift
        for r in range(levels - 1):
            value = prod_all[it, r] * value + shift_all[it, r]
        solved[it, 0] = value
        for k in range(1, GROUP):
            value = decay_all[it, k - 1] * value + offset_all[it, k - 1]
            solved[it, k] = value
        @pl.when(more & low & has_up)
        def _():
            start_all(halo_copies(it, 0))

        @pl.when(more & high & has_down)
        def _():
            start_all(halo_copies(it, 1))

        start_all(back_copies(it))
        field[it + 1, mine] = solved[it, g]
        back_all(it).wait_recv()

        @pl.when(more & has_down)
        def _():
            halo_here(it, 0).wait_recv()

        @pl.when(more & has_up)
        def _():
            halo_here(it, 1).wait_recv()

        group_all(it, 0, decay_all).wait_send()
        group_all(it, 1, offset_all).wait_send()
        level_all(it, 0, prod_all).wait_send()
        level_all(it, 1, shift_all).wait_send()
        back_all(it).wait_send()

        @pl.when(more & low & has_up)
        def _():
            halo_sent(it, 0).wait_send()

        @pl.when(more & high & has_down)
        def _():
            halo_sent(it, 1).wait_send()

        return 0

    lax.fori_loop(0, ITERS, sweep, 0)

    ends_out[0] = field[ITERS, own]
    end_copy().wait_recv()
    ends_out[1] = end_prev[...]
    end_copy().wait_send()


def solution(mesh):
    slices, strips = mesh.shape["tm"], mesh.shape["space"]

    def on_device(start_states, region_map, source, front):
        _, rows, cols = start_states.shape
        slab = rows // GROUP
        levels = slices // GROUP
        up_base = rows if strips <= 2 else rows + FINE
        total_rows = up_base + FINE
        f32 = jnp.float32
        dma = pltpu.SemaphoreType.DMA
        vmem = pl.BlockSpec(memory_space=pltpu.VMEM)
        shapes = [
            ((total_rows, cols), f32),
            ((total_rows, cols), jnp.int32),
            ((2, total_rows, cols), f32),
        ]
        wide = pl.pallas_call(
            functools.partial(edge_kernel, strips, rows, up_base),
            out_shape=[jax.ShapeDtypeStruct(*shape) for shape in shapes],
            in_specs=[pl.BlockSpec(memory_space=pltpu.HBM)] * 3,
            out_specs=[vmem] * 3,
            scratch_shapes=[pltpu.VMEM(*shape) for shape in shapes]
            + [dma((3,)), dma((2, 3)), dma((2, 3))],
            compiler_params=pltpu.CompilerParams(
                collective_id=0, has_side_effects=True, vmem_limit_bytes=16 * 2**20
            ),
        )(*(
            pltpu.with_memory_space_constraint(a, pltpu.HBM)
            for a in (start_states, region_map, source)
        ))
        ends = pl.pallas_call(
            functools.partial(kernel, slices, strips, rows, cols, up_base, total_rows),
            out_shape=jax.ShapeDtypeStruct((2, rows, cols), f32),
            in_specs=[vmem] * 3 + [pl.BlockSpec(memory_space=pltpu.SMEM)],
            out_specs=vmem,
            scratch_shapes=[
                pltpu.VMEM((ITERS + 1, total_rows, cols), f32),
                pltpu.VMEM((4, total_rows, cols), f32),
                pltpu.VMEM((4, total_rows, cols), f32),
                pltpu.VMEM((2, total_rows, cols), f32),
                pltpu.VMEM((ITERS, rows, cols), f32),
                pltpu.VMEM((ITERS, GROUP, slab, cols), f32),
                pltpu.VMEM((ITERS, rows, cols), f32),
                pltpu.VMEM((ITERS, GROUP, slab, cols), f32),
                pltpu.VMEM((ITERS, slab, cols), f32),
                pltpu.VMEM((ITERS, levels - 1, slab, cols), f32),
                pltpu.VMEM((ITERS, slab, cols), f32),
                pltpu.VMEM((ITERS, levels - 1, slab, cols), f32),
                pltpu.VMEM((ITERS, GROUP, slab, cols), f32),
                pltpu.VMEM((rows, cols), f32),
                pltpu.VMEM((rows, cols), f32),
                dma((ITERS, 2)),
                dma((ITERS, 2)),
                dma((ITERS, 2)),
                dma((ITERS, 2)),
                dma((ITERS,)),
                dma((ITERS,)),
                dma((ITERS, 2)),
                dma((ITERS, 2)),
                dma,
                dma,
            ],
            compiler_params=pltpu.CompilerParams(
                collective_id=1, has_side_effects=True, vmem_limit_bytes=16 * 2**20
            ),
        )(*wide, jnp.reshape(front, (1,)))
        return ends[0:1], ends[1:2] - ends[0:1]

    placed = (P("tm", "space", None), P("space", None), P(None, "space", None), P())
    return jax.shard_map(
        on_device,
        mesh=mesh,
        in_specs=placed,
        out_specs=(P("tm", "space", None), P("tm", "space", None)),
        check_vma=False,
    )
```

profile of v0, /device:TPU:0, one launch (start us, length us, event | category | flops | bytes accessed | tf_op | source)
XLA Modules:
  0.0 37.8 jit_solution(11033684212070065951)
XLA Ops:
  1.3 6.2 %shard_map.59 = (f32[48,256]{1,0:T(8,128)S(1)}, s32[48,256]{1,0:T(8,128)S(1)}, f32[2,48,256]{2,1,0:T(8,128)S(1)}) custom-call(f32[1,32,256]{2,1,0:T(8,128)} %states_in.1, s32[32,256]{1,0:T(8,128)} %region_in.1, f32[2,32,256]{2,1,0:T(8,128)} %source_in.1), custom_call_target="tpu_custom_call" | custom-call | tf_op jit(solution)/shard_map/pallas_call | solution.py:491
  7.5 29.6 %shard_map.60 = f32[2,32,256]{2,1,0:T(8,128)S(1)} custom-call(f32[48,256]{1,0:T(8,128)S(1)} %get-tuple-element.5.begin, s32[48,256]{1,0:T(8,128)S(1)} %get-tuple-element.6.region, f32[2,48,256]{2,1,0:T(8,128)S(1)} %get-tuple-element.7.source, s32[1]{0:T(128)} %bitcast.1.front_ref), custom_call_target="tpu_custom_call" | custom-call | tf_op jit(solution)/shard_map/pallas_call | solution.py:505
  37.1 0.6 %slice_subtract_fusion = (f32[1,32,256]{2,1,0:T(8,128)}, f32[1,32,256]{2,1,0:T(8,128)}) fusion(f32[2,32,256]{2,1,0:T(8,128)S(1)} %shard_map.60), kind=kLoop, calls=%fused_computation | loop fusion | flops 8192 | bytes 131072 | tf_op jit(solution)/shard_map/sub | solution.py:541
where the time goes:
time: 38 us; the launch traced here: 37.8 us
  Pallas kernels  35.9 us (94%)
  between operations  1.29 us (3%)
  other arithmetic  0.63 us (2%)
    pallas_call x1, Pallas kernels, on_device(): pl.pallas_call(functools.partial(kernel, slices, strips, rows, cols, up_b...  29.6 us
    pallas_call x1, Pallas kernels, on_device(): pl.pallas_call(functools.partial(edge_kernel, strips, rows, up_base), out...  6.24 us

commit v1 on v0

--- a/solution.py
+++ b/solution.py
@@ -11,8 +11,9 @@
 FINE = 16
 ITERS = 2
 GROUP = 4
-DECAY_AT = 5
-PRODUCT_AT = 11
+PAIR = 2
+DECAY_AT = 2
+PRODUCT_AT = 5
 TILE = 8
 LANES = 128
 
@@ -371,6 +372,9 @@
         def turn(k, carry):
             v, cos_k, sin_k = carry
             v, diagonals = step(nest(v), cos_k, sin_k)
+            for _ in range(1, PAIR):
+                cos_k, sin_k = cos_k * cos_d - sin_k * sin_d, sin_k * cos_d + cos_k * sin_d
+                v, _ = step(v, cos_k, sin_k)
 
             @pl.when(k == 0)
             def _():
@@ -398,7 +402,7 @@
 
             return flat(v), cos_k * cos_d - sin_k * sin_d, sin_k * cos_d + cos_k * sin_d
 
-        v, _, _ = lax.fori_loop(0, FINE, turn, (flat(tiles(field.at[it], groups)), cos0, sin0))
+        v, _, _ = lax.fori_loop(0, FINE // PAIR, turn, (flat(tiles(field.at[it], groups)), cos0, sin0))
         v = nest(v)
         for r in range(own_groups):
             for h in range(halves):
@@ -447,6 +451,17 @@
         def _():
             halo_here(it, 1).wait_recv()
 
+        return 0
+
+    lax.fori_loop(0, ITERS, sweep, 0)
+
+    ends_out[0] = field[ITERS, own]
+    end_copy().wait_recv()
+    ends_out[1] = end_prev[...]
+    end_copy().wait_send()
+
+    def settle(it, _):
+        more = it < ITERS - 1
         group_all(it, 0, decay_all).wait_send()
         group_all(it, 1, offset_all).wait_send()
         level_all(it, 0, prod_all).wait_send()
@@ -463,12 +478,7 @@
 
         return 0
 
-    lax.fori_loop(0, ITERS, sweep, 0)
-
-    ends_out[0] = field[ITERS, own]
-    end_copy().wait_recv()
-    ends_out[1] = end_prev[...]
-    end_copy().wait_send()
+    lax.fori_loop(0, ITERS, settle, 0)
 
 
 def solution(mesh):

time: 38 us -> 37.7 us (level)
  no operation moved by 1% of the time
where the time goes in v1:
time: 37.7 us; the launch traced here: 37.6 us
  Pallas kernels  35.7 us (95%)
  between operations  1.29 us (3%)
  other arithmetic  0.63 us (2%)
    pallas_call x1, Pallas kernels, on_device(): pl.pallas_call(functools.partial(kernel, slices, strips, rows, cols, up_b...  29.4 us
    pallas_call x1, Pallas kernels, on_device(): pl.pallas_call(functools.partial(edge_kernel, strips, rows, up_base), out...  6.24 us

profile of v1, /device:TPU:0, one launch (start us, length us, event | category | flops | bytes accessed | tf_op | source)
XLA Modules:
  0.0 37.6 jit_solution(15746899973274862962)
XLA Ops:
  1.3 6.2 %shard_map.59 = (f32[48,256]{1,0:T(8,128)S(1)}, s32[48,256]{1,0:T(8,128)S(1)}, f32[2,48,256]{2,1,0:T(8,128)S(1)}) custom-call(f32[1,32,256]{2,1,0:T(8,128)} %states_in.1, s32[32,256]{1,0:T(8,128)} %region_in.1, f32[2,32,256]{2,1,0:T(8,128)} %source_in.1), custom_call_target="tpu_custom_call" | custom-call | tf_op jit(solution)/shard_map/pallas_call | solution.py:501
  7.5 29.4 %shard_map.60 = f32[2,32,256]{2,1,0:T(8,128)S(1)} custom-call(f32[48,256]{1,0:T(8,128)S(1)} %get-tuple-element.5.begin, s32[48,256]{1,0:T(8,128)S(1)} %get-tuple-element.6.region, f32[2,48,256]{2,1,0:T(8,128)S(1)} %get-tuple-element.7.source, s32[1]{0:T(128)} %bitcast.1.front_ref), custom_call_target="tpu_custom_call" | custom-call | tf_op jit(solution)/shard_map/pallas_call | solution.py:515
  36.9 0.6 %slice_subtract_fusion = (f32[1,32,256]{2,1,0:T(8,128)}, f32[1,32,256]{2,1,0:T(8,128)}) fusion(f32[2,32,256]{2,1,0:T(8,128)S(1)} %shard_map.60), kind=kLoop, calls=%fused_computation | loop fusion | flops 8192 | bytes 131072 | tf_op jit(solution)/shard_map/sub | solution.py:551

commit v2 on v1

--- a/solution.py
+++ b/solution.py
@@ -12,8 +12,8 @@
 ITERS = 2
 GROUP = 4
 PAIR = 2
-DECAY_AT = 2
-PRODUCT_AT = 5
+DECAY_AT = 4
+PRODUCT_AT = 6
 TILE = 8
 LANES = 128
 
@@ -174,22 +174,23 @@
 
     expected = (GROUP - 1) + (levels - 1) + 2
 
-    @pl.when(has_up)
-    def _():
-        for j in range(GROUP):
-            greet(peer(j), x - 1)
-
-    @pl.when(has_down)
-    def _():
-        for j in range(GROUP):
-            greet(peer(j), x + 1)
-
-    for j in range(1, GROUP):
-        greet(peer(j), x)
     for i in range(1, levels):
         greet(far(i), x)
     greet((t + 1) % slices, x)
     greet((t + slices - 1) % slices, x)
+
+    @pl.when(has_up)
+    def _():
+        for j in range(GROUP):
+            greet(peer(j), x - 1)
+
+    @pl.when(has_down)
+    def _():
+        for j in range(GROUP):
+            greet(peer(j), x + 1)
+
+    for j in range(1, GROUP):
+        greet(peer(j), x)
 
     own = pl.ds(0, rows)
     cos0, sin0 = jnp.float32(1.0), jnp.float32(0.0)

time: 37.7 us -> 37.7 us (level)
  no operation moved by 1% of the time
where the time goes in v2:
time: 37.7 us; the launch traced here: 37.5 us
  Pallas kernels  35.6 us (94%)
  between operations  1.29 us (3%)
  other arithmetic  0.63 us (2%)
    pallas_call x1, Pallas kernels, on_device(): pl.pallas_call(functools.partial(kernel, slices, strips, rows, cols, up_b...  29.3 us
    pallas_call x1, Pallas kernels, on_device(): pl.pallas_call(functools.partial(edge_kernel, strips, rows, up_base), out...  6.24 us

profile of v2, /device:TPU:0, one launch (start us, length us, event | category | flops | bytes accessed | tf_op | source)
XLA Modules:
  0.0 37.5 jit_solution(13157142829031833945)
XLA Ops:
  1.3 6.2 %shard_map.59 = (f32[48,256]{1,0:T(8,128)S(1)}, s32[48,256]{1,0:T(8,128)S(1)}, f32[2,48,256]{2,1,0:T(8,128)S(1)}) custom-call(f32[1,32,256]{2,1,0:T(8,128)} %states_in.1, s32[32,256]{1,0:T(8,128)} %region_in.1, f32[2,32,256]{2,1,0:T(8,128)} %source_in.1), custom_call_target="tpu_custom_call" | custom-call | tf_op jit(solution)/shard_map/pallas_call | solution.py:502
  7.5 29.3 %shard_map.60 = f32[2,32,256]{2,1,0:T(8,128)S(1)} custom-call(f32[48,256]{1,0:T(8,128)S(1)} %get-tuple-element.5.begin, s32[48,256]{1,0:T(8,128)S(1)} %get-tuple-element.6.region, f32[2,48,256]{2,1,0:T(8,128)S(1)} %get-tuple-element.7.source, s32[1]{0:T(128)} %bitcast.1.front_ref), custom_call_target="tpu_custom_call" | custom-call | tf_op jit(solution)/shard_map/pallas_call | solution.py:516
  36.9 0.6 %slice_subtract_fusion = (f32[1,32,256]{2,1,0:T(8,128)}, f32[1,32,256]{2,1,0:T(8,128)}) fusion(f32[2,32,256]{2,1,0:T(8,128)S(1)} %shard_map.60), kind=kLoop, calls=%fused_computation | loop fusion | flops 8192 | bytes 131072 | tf_op jit(solution)/shard_map/sub | solution.py:552
